TPU v7x, 768 devices: a whole 4x8x12 slice. The times are simulated.
768 devices in a mesh: dp: 96 (over x, z_hi, y), tensor: 8 (over z_lo, core).
Axes of the slice: x: 4, y: 8, z: 12 (z_hi: 3, z_lo: 4; z = z_hi * 4 + z_lo), core: 2. Of those that a mesh axis runs over, the one named last changes fastest.
Arguments:
- layer_input: bfloat16 [49152, 4608], P('dp'), may hold values from -6 to 6
- key_grad: bfloat16 [49152, 1024], P('dp', 'tensor'), may hold values from -0.25 to 0.25
- key_weight: bfloat16 [4608, 1024], P(None, 'tensor'), may hold values from -4.21875 to 4.21875
- error_state: bfloat16 [96, 4608, 1024], P('dp', None, 'tensor'), may hold values from -6 to 6
- q_start: float32 [1024, 32], P('tensor'), may hold values from -6 to 6
Outputs:
- error_next: bfloat16 [96, 4608, 1024], P('dp', None, 'tensor')
- input_grad: bfloat16 [49152, 4608], P(('dp', 'tensor'))
- p_factor: float32 [8, 4608, 32], P('tensor')
- q_factor: float32 [1024, 32], P('tensor')
All inputs are finite; a program needn't handle non-finite values.
Results may differ from a plain program's by a relative error of at most 0.017.
Values may be sent and summed in bfloat16 or wider, within the bound.
A program may use at most 64 MiB of HBM per device.

v0:
```python
import jax
import jax.numpy as jnp
from jax import lax
from jax.sharding import PartitionSpec as P


def orthonormal(left, gram):
    lower = jnp.linalg.cholesky(gram)
    return lax.linalg.triangular_solve(lower, left, left_side=False, lower=True, transpose_a=True)


def shards(layer_input, key_grad, key_weight, error_state, q_start):
    partial_value = jnp.dot(key_grad, key_weight.T, preferred_element_type=jnp.float32)
    input_grad = lax.psum_scatter(
        partial_value.astype(jnp.bfloat16), "tensor", scatter_dimension=0, tiled=True
    )
    merged = jnp.einsum("td,tk->dk", layer_input, key_grad, preferred_element_type=jnp.float32)
    merged = merged + error_state[0].astype(jnp.float32)
    left = jnp.dot(merged, q_start, precision=lax.Precision.HIGHEST)
    summed = lax.psum(left, "dp")
    gram = jnp.dot(summed.T, summed, precision=lax.Precision.HIGHEST)
    p_factor = orthonormal(summed, gram)
    right = jnp.einsum("dk,dr->kr", merged, p_factor, precision=lax.Precision.HIGHEST)
    q_mean = lax.psum(right, "dp") / lax.axis_size("dp")
    approx = jnp.dot(p_factor, q_mean.T, precision=lax.Precision.HIGHEST)
    error_next = (merged - approx).astype(jnp.bfloat16)
    return (error_next[None], input_grad, p_factor[None], q_mean)


def solution(mesh):
    return jax.shard_map(
        shards,
        mesh=mesh,
        in_specs=(
            P("dp", None),
            P("dp", "tensor"),
            P(None, "tensor"),
            P("dp", None, "tensor"),
            P("tensor", None),
        ),
        out_specs=(
            P("dp", None, "tensor"),
            P(("dp", "tensor"), None),
            P("tensor", None, None),
            P("tensor", None),
        ),
        check_vma=False,
    )
```

profile of v0, /device:TPU:64, one launch (start us, length us, event | category | flops | bytes accessed | tf_op | source)
XLA Modules:
  0.0 1924.7 jit_solution(3065992213769522488)
XLA Ops:
  8.0 0.0 copy-start
  8.0 0.0 copy-start.3
  8.0 0.0 all-reduce.2.cloned.1.call-start
  8.1 4.3 convolution_add_fusion
  12.3 0.0 copy-done.3
  12.3 3.3 fusion.6
  15.6 0.0 all-reduce.2.cloned.1.call-update
  15.6 0.0 reduce-scatter.2.cloned.1.call-start
  15.7 0.0 copy-done
  15.7 4.4 convolution_convert_fusion
  20.1 0.0 reduce-scatter.2.cloned.1.call-update
  20.1 1230.8 %all-reduce.2.cloned.1.call-done = f32[4608,32]{0,1:T(8,128)} async-done(((f32[4608,32]{0,1:T(8,128)}), f32[4608,32]{0,1:T(8,128)}) %all-reduce.2.cloned.1.call-update) | async-done | bytes 589840 | tf_op jit(solution)/shard_map/psum | solution.py:20
  1250.9 1.8 fusion.7
  1252.8 0.7 copy.9
  1253.5 1.3 fusion.5
  1254.8 3.6 cholesky.16
  1258.5 0.6 compare_reduce_fusion
  1259.1 1.3 fusion.2
  1260.4 3.2 custom-call.6
  1263.5 1.8 fusion.3
  1265.3 0.0 copy-start.1
  1265.3 0.8 copy-done.1
  1266.1 1.5 fusion.8
  1267.6 643.0 %psum.15 = f32[128,32]{0,1:T(8,128)} all-reduce(f32[128,32]{0,1:T(8,128)S(1)} %fusion.8), channel_id=1, replica_groups=mesh['dp'=96,'tensor'=8] {'dp'}, use_global_device_ids=true, to_apply=%region_3.4 | all-reduce | flops 4096 | bytes 32768 | tf_op jit(solution)/shard_map/psum | solution.py:24
  1910.6 0.7 broadcast_multiply_fusion
  1911.3 0.0 copy-start.2
  1911.3 5.9 fusion.1
  1917.2 0.0 reduce-scatter.2.cloned.1.call-done
  1917.2 0.0 copy-done.2
  (1 shorter events, 0.0 us)
Async XLA Ops:
  8.0 7.7 copy-start
  8.0 4.3 copy-start.3
  8.0 1242.9 %all-reduce.2.cloned.1.call-start = ((), (), s32[]{:S(2)}) async-start(), calls=%async_computation.1 | async-start | bytes 1179648 | tf_op jit(solution)/shard_map/psum | solution.py:20
  15.6 1901.6 %reduce-scatter.2.cloned.1.call-start = ((), (), s32[]{:S(2)}) async-start(), calls=%async_computation.2 | async-start | bytes 5308416 | tf_op jit(solution)/shard_map/reduce_scatter | solution.py:14
  1265.3 0.8 copy-start.1
  1911.3 5.9 copy-start.2
Sparse Core Ops, SparseCore 0:
  15.8 1235.1 all-reduce.1
Sparse Core Ops, SparseCore 1:
  20.2 68.5 reduce-scatter.1
where the time goes:
time: 1930 us; the launch traced here: 1920 us
  waiting for transfers between devices  1230 us (64%)
  blocking collectives  643 us (33%)
  matrix products  22.9 us (1%)
    psum x1, waiting for transfers between devices, shards(): summed = lax.psum(left, 'dp')  1230 us
    psum x1, blocking collectives, shards(): q_mean = lax.psum(right, 'dp') / lax.axis_size('dp')  643 us
  transfers between devices with their start and end apart: 2, of which 1 were waited for; matrix products, arithmetic and copies ran while one was open for 1% of the time, Pallas kernels for 0%

commit v1 on v0

v1 whole, which is shorter than its diff:
```python
import functools

import jax
import jax.numpy as jnp
from jax import lax
from jax.experimental import pallas as pl
from jax.experimental.pallas import tpu as pltpu
from jax.sharding import PartitionSpec as P

MESH = pl.DeviceIdType.MESH
F32, BF16 = jnp.float32, jnp.bfloat16
NX, NZH, NY, NZL, NC = 4, 3, 8, 4, 2
D, R, KD, TOK = 4608, 32, 128, 512
XC = D // NX
HALF = 640
SL = D // 4
HIGH = lax.Precision.HIGHEST
NT = (((1,), (1,)), ((), ()))
TN = (((0,), (0,)), ((), ()))
NN = (((1,), (0,)), ((), ()))


def mm(a, b, dims, precision=None):
    return lax.dot_general(a, b, dims, precision=precision, preferred_element_type=F32)


def split(a):
    hi = a.astype(BF16)
    return hi, (a - hi.astype(F32)).astype(BF16)


def device(x, y, z, c):
    return ((x * NZH + z // NZL) * NY + y, lax.rem(z, NZL) * NC + c)


def kernel(x_hbm, g_hbm, w_hbm, e_hbm, qt_hbm,
           err_out, ig_out, pt_out, qf_out,
           xv, gv, ev, qv, wbuf, gbuf, igres, igbuf,
           ploc, ra, pa, rb, rc, pd, pe, mhi, mlo, rx, rz, ry, aug, pf, at, err,
           lsem, sa, da, sb, db, sc, dc, sd, dd, se, de,
           sx, dx, sz, dz, sy, dy, sw, dw, sg, dg, sr, dr, so, do, osem):
    dp, t = lax.axis_index("dp"), lax.axis_index("tensor")
    x, zh, y = dp // (NZH * NY), lax.rem(dp // NY, NZH), lax.rem(dp, NY)
    zl, c = t // NC, lax.rem(t, NC)
    z = zh * NZL + zl
    oc = 1 - c
    yb = lax.rem(y, 2)
    yp = y + 1 - 2 * yb

    def zdev(k, core):
        return device(x, y, lax.rem(z + k + 12, 12), core)

    def xdev(k):
        return device(lax.rem(x + k, NX), y, z, c)

    def ydev(k):
        return device(x, lax.rem(y + k, NY), z, c)

    def gdev(k):
        return device(x, y, zh * NZL + lax.rem(zl + k, NZL), c)

    other, part, partother = device(x, y, z, oc), device(x, yp, z, c), device(x, yp, z, oc)

    def remote(src, dst, ssem, rsem, dev):
        return pltpu.make_async_remote_copy(src, dst, ssem, rsem, device_id=dev, device_id_type=MESH)

    loads = [pltpu.make_async_copy(g_hbm, gv, lsem.at[0]), pltpu.make_async_copy(qt_hbm, qv, lsem.at[1]),
             pltpu.make_async_copy(e_hbm, ev, lsem.at[2])]
    for l in loads:
        l.start()

    def xload(k):
        cols = pl.ds(pl.multiple_of(lax.rem(x + k, NX) * XC, 128), XC)
        return pltpu.make_async_copy(x_hbm.at[:, cols], xv.at[:, cols], lsem.at[3 + k % 4])
    for k in (1, 2, 3, 4):
        xload(k).start()
    wcol = pl.multiple_of((c * NZL + zl) * KD, KD)
    wrow = lambda core, off=0: pl.multiple_of((yb * 2 + core) * SL + off, 64)
    wown = pltpu.make_async_copy(w_hbm.at[pl.ds(wrow(c), SL)], wbuf.at[:, pl.ds(wcol, KD)], lsem.at[7])
    wown.start()

    barrier = pltpu.get_barrier_semaphore()
    greet = ([xdev(k) for k in (1, 2, 3)] + [ydev(k) for k in range(1, 8)] + [zdev(k, c) for k in (4, -4)]
             + [gdev(k) for k in (1, 2, 3)] + [zdev(k, cc) for k in (1, -1, 2, -2) for cc in (0, 1)] + [other, partother])
    for d in greet:
        pl.semaphore_signal(barrier, inc=1, device_id=d, device_id_type=MESH)

    loads[0].wait()
    loads[1].wait()
    qh, ql = split(qv[...])
    q2 = jnp.concatenate([qh, ql], axis=0)
    gq = mm(q2, gv[...], NT)
    gh, gl = split(gq[:R] + gq[R:])
    g2 = jnp.concatenate([gh, gl], axis=0)

    pl.semaphore_wait(barrier, len(greet))

    gsend = [remote(gv.at[pl.ds(pl.multiple_of(lax.rem(zl + k, NZL) * 128, 128), 128)], gbuf.at[0, :, pl.ds(wcol, KD)],
                    sg.at[k - 1], dg.at[k - 1], gdev(k)) for k in (1, 2, 3)]
    for s in gsend:
        s.start()
    gbuf[0, :, pl.ds(wcol, KD)] = gv[pl.ds(pl.multiple_of(zl * 128, 128), 128)]
    loads[2].wait()

    asend = []
    for k in (2, 1, 3, 4):
        xload(k).wait()
        ch = lax.rem(x + k, NX)
        base = pl.multiple_of(ch * XC, 128)
        for off in (0, 384, 768):
            r = mm(g2, xv[:, pl.ds(base + off, 384)], NN) + mm(q2, ev[pl.ds(base + off, 384)], NT)
            ploc[ch, :, pl.ds(off, 384)] = r[:R] + r[R:]
        if k < 4:
            a = remote(ploc.at[ch], ra.at[k - 1], sa.at[k - 1], da.at[k - 1], xdev(k))
            a.start()
            asend.append(a)

    wsend = [remote(w_hbm.at[pl.ds(wrow(oc), SL)], wbuf.at[:, pl.ds(wcol, KD)], sw.at[0], dw.at[0], other)]
    i = 1
    for k in (1, -1):
        for cc in (0, 1):
            rel = (cc + c) - 2 * cc * c
            wsend.append(remote(w_hbm.at[pl.ds(wrow(cc), SL)], wbuf.at[:, pl.ds(wcol, KD)],
                                sw.at[i], dw.at[(1 if k == 1 else 3) + rel], zdev(k, cc)))
            i += 1
    for k in (2, -2):
        off = 0 if k == 2 else SL // 2
        for cc in (0, 1):
            rel = (cc + c) - 2 * cc * c
            wsend.append(remote(w_hbm.at[pl.ds(wrow(cc, off), SL // 2)], wbuf.at[pl.ds(off, SL // 2), pl.ds(wcol, KD)],
                                sw.at[i], dw.at[(5 if k == 2 else 7) + rel], zdev(k, cc)))
            i += 1
    for s in wsend:
        s.start()

    def merge(j, carry):
        rows = pl.ds(pl.multiple_of(j * 256, 256), 256)
        m = mm(xv[:, rows], gv[...], TN) + ev[rows].astype(F32)
        h, l = split(m)
        mhi[rows] = h
        mlo[rows] = l
        return carry
    lax.fori_loop(0, 18, merge, 0)

    for s in asend:
        s.wait_recv()
    tot = ploc[x] + ra[0] + ra[1] + ra[2]
    pa[0] = tot[:, :HALF]
    pa[1, :, pl.ds(0, XC - HALF)] = tot[:, HALF:]
    pa[1, :, pl.ds(XC - HALF, 2 * HALF - XC)] = jnp.zeros((R, 2 * HALF - XC), F32)

    def piece(ref, j):
        return ref.at[j // 4, pl.ds(pl.multiple_of(lax.rem(j, 4) * 8, 8), 8)]

    bsend = []
    for k in range(1, 8):
        b = remote(piece(pa, lax.rem(y + k, NY)), rb.at[k - 1], sb.at[k - 1], db.at[k - 1], ydev(k))
        b.start()
        bsend.append(b)

    for s in gsend:
        s.wait_recv()
    half = pl.ds(pl.multiple_of(c * 512, 512), 512)
    rsend = [remote(gbuf.at[0, :, half], gbuf.at[i, :, half], sr.at[k], dr.at[k], d)
             for k, (i, d) in enumerate([(0, other), (1, part), (1, partother)])]
    for s in rsend:
        s.start()

    for s in bsend:
        s.wait_recv()
    own = piece(pa, y)[...]
    for k in range(7):
        own = own + rb[k]
    rc[zh] = own

    csend = []
    for k, dz_ in ((0, 4), (1, -4)):
        b = remote(rc.at[zh], rc.at[zh], sc.at[k], dc.at[k], zdev(dz_, c))
        b.start()
        csend.append(b)
    for s in csend:
        s.wait_recv()
    piece(pd, y)[...] = rc[0] + rc[1] + rc[2]

    dsend = []
    for k in range(1, 8):
        b = remote(piece(pd, y), piece(pd, y), sd.at[k - 1], dd.at[k - 1], ydev(k))
        b.start()
        dsend.append(b)
    for s in dsend:
        s.wait_recv()

    pe[x] = pd[...]
    esend = []
    for k in (2, 1, 3):
        b = remote(pd, pe.at[x], se.at[k - 1], de.at[k - 1], xdev(k))
        b.start()
        esend.append(b)

    def right(ch):
        tot = jnp.zeros((R, KD), F32)
        for h, n in ((0, HALF), (1, XC - HALF)):
            ph, pl_ = split(pe[ch, h, :, :n])
            rows = pl.ds(pl.multiple_of(ch * XC + h * HALF, 128), n)
            r = mm(jnp.concatenate([ph, pl_], axis=0), mhi[rows], NN)
            tot = tot + r[:R] + r[R:] + mm(ph, mlo[rows], NN)
        return tot

    qp = right(x)
    for k, s in ((1, esend[1]), (3, esend[2]), (2, esend[0])):
        s.wait_recv()
        qp = qp + right(lax.rem(x + 4 - k, NX))

    rx[x] = qp
    fsend = []
    for k in (1, 2, 3):
        b = remote(rx.at[x], rx.at[x], sx.at[k - 1], dx.at[k - 1], xdev(k))
        b.start()
        fsend.append(b)

    gram = jnp.zeros((R, R), F32)
    for ch in range(NX):
        for h, n in ((0, HALF), (1, XC - HALF)):
            b = pe[ch, h, :, :n]
            gram = gram + mm(b, b, NT, HIGH)
    row = lax.broadcasted_iota(jnp.int32, (R, KD), 0)
    col = lax.broadcasted_iota(jnp.int32, (R, KD), 1)
    aug[...] = jnp.where(col == row + R, 1.0, 0.0)
    aug[:, :R] = gram

    def factor(k, carry):
        a = aug[...]
        r = jnp.sum(jnp.where(row == k, a, 0.0), axis=0, keepdims=True)
        cl = jnp.sum(jnp.where(col == k, a, 0.0), axis=1, keepdims=True)
        pivot = jnp.sum(jnp.where(col[:1] == k, r, 0.0), axis=1, keepdims=True)
        s = 1.0 / jnp.sqrt(pivot)
        rn = r * s
        aug[...] = jnp.where(row == k, rn, jnp.where(row > k, a - (cl * s) * rn, a))
        return carry

    for s in fsend:
        s.wait_recv()
    rz[zh] = rx[0] + rx[1] + rx[2] + rx[3]

    hsend = []
    for k, dz_ in ((0, 4), (1, -4)):
        b = remote(rz.at[zh], rz.at[zh], sz.at[k], dz.at[k], zdev(dz_, c))
        b.start()
        hsend.append(b)
    lax.fori_loop(0, 16, factor, 0)
    for s in hsend:
        s.wait_recv()
    ry[y] = rz[0] + rz[1] + rz[2]

    ysend = []
    for k in range(1, 8):
        b = remote(ry.at[y], ry.at[y], sy.at[k - 1], dy.at[k - 1], ydev(k))
        b.start()
        ysend.append(b)
    lax.fori_loop(16, R, factor, 0)
    linv = aug[:, R:2 * R]
    for ch in range(NX):
        for h, n in ((0, HALF), (1, XC - HALF)):
            cols = pl.ds(ch * XC + h * HALF, n)
            p = mm(linv, pe[ch, h, :, :n], NN, HIGH)
            pf[:, cols] = p
            ph, pl_ = split(p)
            at[pl.ds(0, R), cols] = ph
            at[pl.ds(R, R), cols] = pl_
            at[pl.ds(2 * R, R), cols] = ph
    at[pl.ds(3 * R, R)] = jnp.zeros((R, D), BF16)
    pout = pltpu.make_async_copy(pf, pt_out, osem.at[0])
    pout.start()
    for s in ysend:
        s.wait_recv()
    q = ry[0]
    for k in range(1, 8):
        q = q + ry[k]
    qf = mm(linv, q, NN, HIGH) * (1.0 / (NX * NY * NZH))
    qf_out[...] = qf
    bh, bl = split(qf)
    b4 = jnp.concatenate([bh, bh, bl, jnp.zeros_like(bl)], axis=0)

    def finish(j, carry):
        rows = pl.ds(pl.multiple_of(j * 256, 256), 256)
        a = mm(at[:, rows], b4, TN)
        err[rows] = ((mhi[rows].astype(F32) - a) + mlo[rows].astype(F32)).astype(BF16)
        return carry
    lax.fori_loop(0, 18, finish, 0)
    eout = pltpu.make_async_copy(err, err_out, osem.at[1])
    eout.start()

    for s in rsend:
        s.wait_recv()
    wown.wait()
    for s in wsend:
        s.wait_recv()

    def grad(j, carry):
        rows = pl.ds(pl.multiple_of(j * 384, 128), 384)
        for b in range(2):
            igres[pl.ds(b * 128, 128), rows] = mm(gbuf[b], wbuf[rows], NT).astype(BF16)
        return carry
    lax.fori_loop(0, 3, grad, 0)
    scol = pl.ds(pl.multiple_of((yb * 2 + c) * SL, 128), SL)
    osend = []
    for k, (b, core, d) in enumerate([(0, oc, other), (1, c, part), (1, oc, partother)]):
        s = remote(igres.at[pl.ds(pl.multiple_of(b * 128 + core * 64, 64), 64)], igbuf.at[:, scol], so.at[k], do.at[k], d)
        s.start()
        osend.append(s)
    igbuf[:, scol] = igres[pl.ds(pl.multiple_of(c * 64, 64), 64)]
    for s in osend:
        s.wait_recv()
    iout = pltpu.make_async_copy(igbuf, ig_out, osem.at[2])
    iout.start()
    for s in asend + bsend + csend + dsend + esend + fsend + hsend + ysend + wsend + gsend + rsend + osend:
        s.wait_send()
    pout.wait()
    eout.wait()
    iout.wait()


def shards(layer_input, key_grad, key_weight, error_state, q_start):
    dma = lambda n: pltpu.SemaphoreType.DMA((n,))
    any_ = pl.BlockSpec(memory_space=pl.ANY)
    err, ig, pt, qt = pl.pallas_call(
        kernel,
        out_shape=(
            jax.ShapeDtypeStruct((D, KD), BF16),
            jax.ShapeDtypeStruct((TOK // 8, D), BF16),
            jax.ShapeDtypeStruct((R, D), F32),
            jax.ShapeDtypeStruct((R, KD), F32),
        ),
        in_specs=[any_] * 5,
        out_specs=(any_, any_, any_, pl.BlockSpec(memory_space=pltpu.VMEM)),
        scratch_shapes=[
            pltpu.VMEM((TOK, D), BF16), pltpu.VMEM((TOK, KD), BF16), pltpu.VMEM((D, KD), BF16), pltpu.VMEM((R, KD), F32),
            pltpu.VMEM((SL, 1024), BF16), pltpu.VMEM((2, 128, 1024), BF16), pltpu.VMEM((256, SL), BF16), pltpu.VMEM((64, D), BF16),
            pltpu.VMEM((NX, R, XC), F32), pltpu.VMEM((3, R, XC), F32), pltpu.VMEM((2, R, HALF), F32),
            pltpu.VMEM((7, 8, HALF), F32), pltpu.VMEM((NZH, 8, HALF), F32), pltpu.VMEM((2, R, HALF), F32),
            pltpu.VMEM((NX, 2, R, HALF), F32), pltpu.VMEM((D, KD), BF16), pltpu.VMEM((D, KD), BF16),
            pltpu.VMEM((NX, R, KD), F32), pltpu.VMEM((NZH, R, KD), F32), pltpu.VMEM((NY, R, KD), F32),
            pltpu.VMEM((R, KD), F32), pltpu.VMEM((R, D), F32), pltpu.VMEM((KD, D), BF16), pltpu.VMEM((D, KD), BF16),
            dma(8), dma(3), dma(3), dma(7), dma(7), dma(2), dma(2), dma(7), dma(7), dma(3), dma(3),
            dma(3), dma(3), dma(2), dma(2), dma(7), dma(7), dma(9), dma(9), dma(3), dma(3), dma(3), dma(3), dma(3), dma(3), dma(3),
        ],
        compiler_params=pltpu.CompilerParams(collective_id=0, has_side_effects=True, vmem_limit_bytes=48 << 20),
        name="powersgd",
    )(layer_input, key_grad, key_weight, error_state[0], q_start.T)
    return (err[None], ig, pt.T[None], qt.T)


def solution(mesh):
    return jax.shard_map(
        shards,
        mesh=mesh,
        in_specs=(
            P("dp", None),
            P("dp", "tensor"),
            P(None, "tensor"),
            P("dp", None, "tensor"),
            P("tensor", None),
        ),
        out_specs=(
            P("dp", None, "tensor"),
            P(("dp", "tensor"), None),
            P("tensor", None, None),
            P("tensor", None),
        ),
        check_vma=False,
    )
```

time: 1930 us -> 99.5 us (0.05)
  waiting for transfers between devices: 1230 us -> 0 us
  blocking collectives: 643 us -> 0 us
  Pallas kernels: 0 us -> 89.9 us
  matrix products: 22.9 us -> 0 us
    psum x1 -> x0, waiting for transfers between devices: 1230 us -> none  [shards(): summed = lax.psum(left, 'dp')]
    psum x1 -> x0, blocking collectives: 643 us -> none  [shards(): q_mean = lax.psum(right, 'dp') / lax.axis_size('dp')]
    pallas_call x0 -> x1, Pallas kernels: none -> 89.9 us  [shards(): pl.pallas_call(kernel, out_shape=(jax.ShapeDtypeStruct((D, KD), BF16), ja...]
    dot_general x6 -> x0, matrix products: 21.2 us -> none  [the longest x1 5.93 us: shards(): approx = jnp.dot(p_factor, q_mean.T, precision=lax.Precision.HIGHEST)]
  transfers between devices with their start and end apart: 2 -> 0, of which waited for: 1 -> 0; matrix products, arithmetic and copies ran while one was open for 1% -> 0% of each run, Pallas kernels for 0% -> 0%
where the time goes in v1:
time: 99.5 us; the launch traced here: 97.9 us
  Pallas kernels  89.9 us (90%)
  local copies, waits for them, and re-layouts  7.4 us (7%)
    pallas_call x1, Pallas kernels, shards(): pl.pallas_call(kernel, out_shape=(jax.ShapeDtypeStruct((D, KD), BF16), ja...  89.9 us
    unnamed x12, local copies, waits for them, and re-layouts  7.4 us

profile of v1, /device:TPU:64, one launch (start us, length us, event | category | flops | bytes accessed | tf_op | source)
XLA Modules:
  0.0 97.9 jit_solution(17365142307303156626)
XLA Ops:
  0.6 0.0 copy-start
  0.6 1.3 %copy-done = bf16[4608,128]{1,0:T(8,128)(2,1)S(1)} copy-done((bf16[4608,128]{1,0:T(8,128)(2,1)S(1)}, bf16[4608,128]{1,0:T(8,128)(2,1)}, u32[]{:S(2)}) %copy-start) | copy-done | bytes 1179672
  1.9 0.0 copy-start.1
  1.9 1.3 %copy-done.1 = bf16[1,4608,128]{2,1,0:T(8,128)(2,1)S(1)} copy-done((bf16[1,4608,128]{2,1,0:T(8,128)(2,1)S(1)}, bf16[1,4608,128]{2,1,0:T(8,128)(2,1)}, u32[]{:S(2)}) %copy-start.1) | copy-done | bytes 1179672
  3.2 0.0 copy-start.2
  3.2 0.9 copy-done.2
  4.1 0.0 copy-start.3
  4.1 0.7 copy-done.3
  4.8 89.9 %powersgd.1 = (bf16[4608,128]{1,0:T(8,128)(2,1)S(1)}, bf16[64,4608]{1,0:T(8,128)(2,1)S(1)}, f32[32,4608]{1,0:T(8,128)S(1)}, f32[32,128]{1,0:T(8,128)S(1)}) custom-call(bf16[512,4608]{1,0:T(8,128)(2,1)} %x_hbm.1, bf16[512,128]{1,0:T(8,128)(2,1)S(1)} %copy-done.2, bf16[4608,128]{1,0:T(8,128)(2,1)S(1)} %copy-done, bf16[4608,128]{1,0:T(8,128)(2,1)S(1)} %bitcast.7, ...), custom_call_target="tpu_custom_call" | custom-call | tf_op jit(solution)/shard_map/powersgd/pallas_call | solution.py:326
  94.7 1.0 %copy.13 = bf16[1,4608,128]{2,1,0:T(8,128)(2,1)} copy(bf16[1,4608,128]{2,1,0:T(8,128)(2,1)S(1)} %bitcast.8) | data formatting | bytes 2359296
  95.7 0.8 copy.14
  96.5 0.8 copy.15
  97.3 0.6 copy.16
Async XLA Ops:
  0.6 1.3 %copy-start = (bf16[4608,128]{1,0:T(8,128)(2,1)S(1)}, bf16[4608,128]{1,0:T(8,128)(2,1)}, u32[]{:S(2)}) copy-start(bf16[4608,128]{1,0:T(8,128)(2,1)} %w_hbm.1) | copy-start | bytes 3538948
  1.9 1.3 %copy-start.1 = (bf16[1,4608,128]{2,1,0:T(8,128)(2,1)S(1)}, bf16[1,4608,128]{2,1,0:T(8,128)(2,1)}, u32[]{:S(2)}) copy-start(bf16[1,4608,128]{2,1,0:T(8,128)(2,1)} %param.8) | copy-start | bytes 3538948
  3.2 0.9 copy-start.2
  4.1 0.7 copy-start.3

commit v2 on v1

--- a/solution.py
+++ b/solution.py
@@ -34,9 +34,9 @@
 
 
 def kernel(x_hbm, g_hbm, w_hbm, e_hbm, qt_hbm,
-           err_out, ig_out, pt_out, qf_out,
+           at_out, mhi_out, mlo_out, ig_out, pf_out, qf_out,
            xv, gv, ev, qv, wbuf, gbuf, igres, igbuf,
-           ploc, ra, pa, rb, rc, pd, pe, mhi, mlo, rx, rz, ry, aug, pf, at, err,
+           ploc, ra, pa, rb, rc, pd, pe, mhi, mlo, rx, rz, ry, aug, pf, at, qf,
            lsem, sa, da, sb, db, sc, dc, sd, dd, se, de,
            sx, dx, sz, dz, sy, dy, sw, dw, sg, dg, sr, dr, so, do, osem):
     dp, t = lax.axis_index("dp"), lax.axis_index("tensor")
@@ -141,6 +141,14 @@
         mlo[rows] = l
         return carry
     lax.fori_loop(0, 18, merge, 0)
+    outs = []
+
+    def put(src, dst):
+        cp = pltpu.make_async_copy(src, dst, osem.at[len(outs)])
+        cp.start()
+        outs.append(cp)
+    put(mhi, mhi_out)
+    put(mlo, mlo_out)
 
     for s in asend:
         s.wait_recv()
@@ -197,6 +205,25 @@
         b.start()
         esend.append(b)
 
+    for s in rsend:
+        s.wait_recv()
+    wown.wait()
+    for s in wsend:
+        s.wait_recv()
+
+    def grad(j, carry):
+        rows = pl.ds(pl.multiple_of(j * 384, 128), 384)
+        for b in range(2):
+            igres[pl.ds(b * 128, 128), rows] = mm(gbuf[b], wbuf[rows], NT).astype(BF16)
+        return carry
+    lax.fori_loop(0, 3, grad, 0)
+    scol = pl.ds(pl.multiple_of((yb * 2 + c) * SL, 128), SL)
+    osend = []
+    for k, (b, core, d) in enumerate([(0, oc, other), (1, c, part), (1, oc, partother)]):
+        s = remote(igres.at[pl.ds(pl.multiple_of(b * 128 + core * 64, 64), 64)], igbuf.at[:, scol], so.at[k], do.at[k], d)
+        s.start()
+        osend.append(s)
+    igbuf[:, scol] = igres[pl.ds(pl.multiple_of(c * 64, 64), 64)]
     def right(ch):
         tot = jnp.zeros((R, KD), F32)
         for h, n in ((0, HALF), (1, XC - HALF)):
@@ -269,70 +296,72 @@
             at[pl.ds(R, R), cols] = pl_
             at[pl.ds(2 * R, R), cols] = ph
     at[pl.ds(3 * R, R)] = jnp.zeros((R, D), BF16)
-    pout = pltpu.make_async_copy(pf, pt_out, osem.at[0])
-    pout.start()
+    put(at, at_out)
+    put(pf, pf_out)
+    for s in osend:
+        s.wait_recv()
+    put(igbuf, ig_out)
     for s in ysend:
         s.wait_recv()
     q = ry[0]
     for k in range(1, 8):
         q = q + ry[k]
-    qf = mm(linv, q, NN, HIGH) * (1.0 / (NX * NY * NZH))
-    qf_out[...] = qf
-    bh, bl = split(qf)
-    b4 = jnp.concatenate([bh, bh, bl, jnp.zeros_like(bl)], axis=0)
-
-    def finish(j, carry):
-        rows = pl.ds(pl.multiple_of(j * 256, 256), 256)
-        a = mm(at[:, rows], b4, TN)
-        err[rows] = ((mhi[rows].astype(F32) - a) + mlo[rows].astype(F32)).astype(BF16)
-        return carry
-    lax.fori_loop(0, 18, finish, 0)
-    eout = pltpu.make_async_copy(err, err_out, osem.at[1])
-    eout.start()
-
-    for s in rsend:
-        s.wait_recv()
-    wown.wait()
-    for s in wsend:
-        s.wait_recv()
-
-    def grad(j, carry):
-        rows = pl.ds(pl.multiple_of(j * 384, 128), 384)
-        for b in range(2):
-            igres[pl.ds(b * 128, 128), rows] = mm(gbuf[b], wbuf[rows], NT).astype(BF16)
-        return carry
-    lax.fori_loop(0, 3, grad, 0)
-    scol = pl.ds(pl.multiple_of((yb * 2 + c) * SL, 128), SL)
-    osend = []
-    for k, (b, core, d) in enumerate([(0, oc, other), (1, c, part), (1, oc, partother)]):
-        s = remote(igres.at[pl.ds(pl.multiple_of(b * 128 + core * 64, 64), 64)], igbuf.at[:, scol], so.at[k], do.at[k], d)
-        s.start()
-        osend.append(s)
-    igbuf[:, scol] = igres[pl.ds(pl.multiple_of(c * 64, 64), 64)]
-    for s in osend:
-        s.wait_recv()
-    iout = pltpu.make_async_copy(igbuf, ig_out, osem.at[2])
-    iout.start()
+    qf[...] = mm(linv, q, NN, HIGH) * (1.0 / (NX * NY * NZH))
+    put(qf, qf_out)
     for s in asend + bsend + csend + dsend + esend + fsend + hsend + ysend + wsend + gsend + rsend + osend:
         s.wait_send()
-    pout.wait()
-    eout.wait()
-    iout.wait()
+    for s in outs:
+        s.wait()
+
+
+def last(at_in, mhi_in, mlo_in, ig_in, pf_in, qf_in, err_out, ig_out, pt_out, qf_out, at, mhi, mlo, qf, ig, pf, err, sem, lsem):
+    def load(a, b, i):
+        cp = pltpu.make_async_copy(a, b, lsem.at[i])
+        cp.start()
+        return cp
+    qload = load(qf_in, qf, 0)
+    loads = []
+    for h in range(3):
+        part = pl.ds(h * 1536, 1536)
+        loads.append([load(at_in.at[:, part], at.at[:, part], 1 + 3 * h), load(mhi_in.at[part], mhi.at[part], 2 + 3 * h),
+                      load(mlo_in.at[part], mlo.at[part], 3 + 3 * h)])
+    through = [(qload, qf, qf_out), (load(ig_in, ig, 10), ig, ig_out), (load(pf_in, pf, 11), pf, pt_out)]
+    copies = [pltpu.make_async_copy(b, o, sem.at[i]) for i, (l, b, o) in enumerate(through)]
+    qload.wait()
+    copies[0].start()
+    bh, bl = split(qf[...])
+    b4 = jnp.concatenate([bh, bh, bl, jnp.zeros_like(bl)], axis=0)
+    for h in range(3):
+        for l in loads[h]:
+            l.wait()
+
+        def finish(j, carry):
+            rows = pl.ds(pl.multiple_of(h * 1536 + j * 256, 256), 256)
+            a = mm(at[:, rows], b4, TN)
+            err[rows] = ((mhi[rows].astype(F32) - a) + mlo[rows].astype(F32)).astype(BF16)
+            return carry
+        lax.fori_loop(0, 6, finish, 0)
+        part = pl.ds(h * 1536, 1536)
+        c = pltpu.make_async_copy(err.at[part], err_out.at[part], sem.at[3 + h])
+        c.start()
+        copies.append(c)
+        if h < 2:
+            through[1 + h][0].wait()
+            copies[1 + h].start()
+    for c in copies:
+        c.wait()
 
 
 def shards(layer_input, key_grad, key_weight, error_state, q_start):
     dma = lambda n: pltpu.SemaphoreType.DMA((n,))
-    any_ = pl.BlockSpec(memory_space=pl.ANY)
-    err, ig, pt, qt = pl.pallas_call(
+    hbm = pl.BlockSpec(memory_space=pltpu.HBM)
+    shape = jax.ShapeDtypeStruct
+    parts = pl.pallas_call(
         kernel,
-        out_shape=(
-            jax.ShapeDtypeStruct((D, KD), BF16),
-            jax.ShapeDtypeStruct((TOK // 8, D), BF16),
-            jax.ShapeDtypeStruct((R, D), F32),
-            jax.ShapeDtypeStruct((R, KD), F32),
-        ),
-        in_specs=[any_] * 5,
-        out_specs=(any_, any_, any_, pl.BlockSpec(memory_space=pltpu.VMEM)),
+        out_shape=(shape((KD, D), BF16), shape((D, KD), BF16), shape((D, KD), BF16),
+                   shape((TOK // 8, D), BF16), shape((R, D), F32), shape((R, KD), F32)),
+        in_specs=[hbm] * 5,
+        out_specs=[hbm] * 6,
         scratch_shapes=[
             pltpu.VMEM((TOK, D), BF16), pltpu.VMEM((TOK, KD), BF16), pltpu.VMEM((D, KD), BF16), pltpu.VMEM((R, KD), F32),
             pltpu.VMEM((SL, 1024), BF16), pltpu.VMEM((2, 128, 1024), BF16), pltpu.VMEM((256, SL), BF16), pltpu.VMEM((64, D), BF16),
@@ -340,13 +369,23 @@
             pltpu.VMEM((7, 8, HALF), F32), pltpu.VMEM((NZH, 8, HALF), F32), pltpu.VMEM((2, R, HALF), F32),
             pltpu.VMEM((NX, 2, R, HALF), F32), pltpu.VMEM((D, KD), BF16), pltpu.VMEM((D, KD), BF16),
             pltpu.VMEM((NX, R, KD), F32), pltpu.VMEM((NZH, R, KD), F32), pltpu.VMEM((NY, R, KD), F32),
-            pltpu.VMEM((R, KD), F32), pltpu.VMEM((R, D), F32), pltpu.VMEM((KD, D), BF16), pltpu.VMEM((D, KD), BF16),
+            pltpu.VMEM((R, KD), F32), pltpu.VMEM((R, D), F32), pltpu.VMEM((KD, D), BF16), pltpu.VMEM((R, KD), F32),
             dma(8), dma(3), dma(3), dma(7), dma(7), dma(2), dma(2), dma(7), dma(7), dma(3), dma(3),
-            dma(3), dma(3), dma(2), dma(2), dma(7), dma(7), dma(9), dma(9), dma(3), dma(3), dma(3), dma(3), dma(3), dma(3), dma(3),
+            dma(3), dma(3), dma(2), dma(2), dma(7), dma(7), dma(9), dma(9), dma(3), dma(3), dma(3), dma(3), dma(3), dma(3), dma(6),
         ],
-        compiler_params=pltpu.CompilerParams(collective_id=0, has_side_effects=True, vmem_limit_bytes=48 << 20),
+        compiler_params=pltpu.CompilerParams(collective_id=0, has_side_effects=True, vmem_limit_bytes=60 << 20),
         name="powersgd",
     )(layer_input, key_grad, key_weight, error_state[0], q_start.T)
+    err, ig, pt, qt = pl.pallas_call(
+        last,
+        out_shape=(shape((D, KD), BF16), shape((TOK // 8, D), BF16), shape((R, D), F32), shape((R, KD), F32)),
+        in_specs=[hbm] * 6,
+        out_specs=[hbm] * 4,
+        scratch_shapes=[pltpu.VMEM((KD, D), BF16), pltpu.VMEM((D, KD), BF16), pltpu.VMEM((D, KD), BF16), pltpu.VMEM((R, KD), F32),
+                        pltpu.VMEM((64, D), BF16), pltpu.VMEM((R, D), F32), pltpu.VMEM((D, KD), BF16), dma(6), dma(12)],
+        compiler_params=pltpu.CompilerParams(vmem_limit_bytes=60 << 20),
+        name="finish",
+    )(*parts)
     return (err[None], ig, pt.T[None], qt.T)
 
 

time: 99.5 us -> 86.6 us (0.87); the launches traced: 97.9 us -> 86.4 us
  local copies, waits for them, and re-layouts: 7.4 us -> 0 us
  Pallas kernels: 89.9 us -> 85.7 us
    unnamed x12 -> x0, local copies, waits for them, and re-layouts: 7.4 us -> none
    pallas_call x1 -> x2, Pallas kernels: 89.9 us -> 85.7 us  [the longest x1 79.9 us: shards(): pl.pallas_call(kernel, out_shape=(shape((KD, D), BF16), shape((D, KD), BF...]
where the time goes in v2:
time: 86.6 us; the launch traced here: 86.4 us
  Pallas kernels  85.7 us (99%)
    pallas_call x1, Pallas kernels, shards(): pl.pallas_call(kernel, out_shape=(shape((KD, D), BF16), shape((D, KD), BF...  79.9 us
    pallas_call x1, Pallas kernels, shards(): pl.pallas_call(last, out_shape=(shape((D, KD), BF16), shape((TOK // 8, D)...  5.81 us

profile of v2, /device:TPU:64, one launch (start us, length us, event | category | flops | bytes accessed | tf_op | source)
XLA Modules:
  0.0 86.4 jit_solution(11702412221431110968)
XLA Ops:
  0.6 79.9 %powersgd.1 = (bf16[128,4608]{1,0:T(8,128)(2,1)}, bf16[4608,128]{1,0:T(8,128)(2,1)}, bf16[4608,128]{1,0:T(8,128)(2,1)}, bf16[64,4608]{1,0:T(8,128)(2,1)}, f32[32,4608]{1,0:T(8,128)}, /*index=5*/f32[32,128]{1,0:T(8,128)}) custom-call(bf16[512,4608]{1,0:T(8,128)(2,1)} %x_hbm.1, bf16[512,128]{1,0:T(8,128)(2,1)} %g_hbm.1, bf16[4608,128]{1,0:T(8,128)(2,1)} %w_hbm.1, ...), custom_call_target="tpu_custom_call" | custom-call | tf_op jit(solution)/shard_map/powersgd/pallas_call | solution.py:359
  80.6 5.8 %finish.1 = (bf16[4608,128]{1,0:T(8,128)(2,1)}, bf16[64,4608]{1,0:T(8,128)(2,1)}, f32[32,4608]{1,0:T(8,128)}, f32[32,128]{1,0:T(8,128)}) custom-call(bf16[128,4608]{1,0:T(8,128)(2,1)} %get-tuple-element.14.at_in, bf16[4608,128]{1,0:T(8,128)(2,1)} %get-tuple-element.15.mhi_in, bf16[4608,128]{1,0:T(8,128)(2,1)} %get-tuple-element.16.mlo_in, ...), custom_call_target="tpu_custom_call" | custom-call | tf_op jit(solution)/shard_map/finish/pallas_call | solution.py:379

commit v3 on v2

--- a/solution.py
+++ b/solution.py
@@ -36,7 +36,7 @@
 def kernel(x_hbm, g_hbm, w_hbm, e_hbm, qt_hbm,
            at_out, mhi_out, mlo_out, ig_out, pf_out, qf_out,
            xv, gv, ev, qv, wbuf, gbuf, igres, igbuf,
-           ploc, ra, pa, rb, rc, pd, pe, mhi, mlo, rx, rz, ry, aug, pf, at, qf,
+           ploc, pown, ra, pa, rb, rc, pd, pb, pe, mhi, mlo, rx, rz, ry, aug, pf, at, qf,
            lsem, sa, da, sb, db, sc, dc, sd, dd, se, de,
            sx, dx, sz, dz, sy, dy, sw, dw, sg, dg, sr, dr, so, do, osem):
     dp, t = lax.axis_index("dp"), lax.axis_index("tensor")
@@ -87,7 +87,18 @@
 
     loads[0].wait()
     loads[1].wait()
-    qh, ql = split(qv[...])
+    row = lax.broadcasted_iota(jnp.int32, (R, KD), 0)
+    col = lax.broadcasted_iota(jnp.int32, (R, KD), 1)
+    q0 = qv[...]
+    aug[...] = jnp.where(col == row + R, 1.0, 0.0)
+    aug[:, :R] = mm(q0, q0, NT, HIGH)
+    a = aug[...]
+    for k in range(R):
+        s = lax.rsqrt(a[k:k + 1, k:k + 1])
+        rn = a[k:k + 1] * s
+        a = jnp.where(row == k, rn, a - jnp.where(row > k, a[:, k:k + 1] * s, 0.0) * rn)
+    aug[...] = a
+    qh, ql = split(mm(aug[:, R:2 * R], q0, NN, HIGH))
     q2 = jnp.concatenate([qh, ql], axis=0)
     gq = mm(q2, gv[...], NT)
     gh, gl = split(gq[:R] + gq[R:])
@@ -109,28 +120,28 @@
         base = pl.multiple_of(ch * XC, 128)
         for off in (0, 384, 768):
             r = mm(g2, xv[:, pl.ds(base + off, 384)], NN) + mm(q2, ev[pl.ds(base + off, 384)], NT)
-            ploc[ch, :, pl.ds(off, 384)] = r[:R] + r[R:]
+            if k < 4:
+                ploc[ch, :, pl.ds(off, 384)] = (r[:R] + r[R:]).astype(BF16)
+            else:
+                pown[:, pl.ds(off, 384)] = r[:R] + r[R:]
         if k < 4:
             a = remote(ploc.at[ch], ra.at[k - 1], sa.at[k - 1], da.at[k - 1], xdev(k))
             a.start()
             asend.append(a)
 
     wsend = [remote(w_hbm.at[pl.ds(wrow(oc), SL)], wbuf.at[:, pl.ds(wcol, KD)], sw.at[0], dw.at[0], other)]
-    i = 1
-    for k in (1, -1):
-        for cc in (0, 1):
-            rel = (cc + c) - 2 * cc * c
-            wsend.append(remote(w_hbm.at[pl.ds(wrow(cc), SL)], wbuf.at[:, pl.ds(wcol, KD)],
-                                sw.at[i], dw.at[(1 if k == 1 else 3) + rel], zdev(k, cc)))
-            i += 1
-    for k in (2, -2):
-        off = 0 if k == 2 else SL // 2
-        for cc in (0, 1):
-            rel = (cc + c) - 2 * cc * c
-            wsend.append(remote(w_hbm.at[pl.ds(wrow(cc, off), SL // 2)], wbuf.at[pl.ds(off, SL // 2), pl.ds(wcol, KD)],
-                                sw.at[i], dw.at[(5 if k == 2 else 7) + rel], zdev(k, cc)))
-            i += 1
-    for s in wsend:
+    for rel, core in ((0, c), (1, oc)):
+        for k in (1, -1):
+            i = (1 if k == 1 else 3) + rel
+            wsend.append(remote(w_hbm.at[pl.ds(wrow(core), SL)], wbuf.at[:, pl.ds(wcol, KD)], sw.at[i], dw.at[i], zdev(k, core)))
+    wpass = []
+    for rel, core in ((0, c), (1, oc)):
+        for k in (1, -1):
+            i = (5 if k == 1 else 7) + rel
+            blk = wbuf.at[pl.ds(0 if k == 1 else SL // 2, SL // 2),
+                          pl.ds(pl.multiple_of((core * NZL + lax.rem(zl + NZL - k, NZL)) * KD, KD), KD)]
+            wpass.append(remote(blk, blk, sw.at[i], dw.at[i], zdev(k, c)))
+    for s in wsend[:3]:
         s.start()
 
     def merge(j, carry):
@@ -152,7 +163,9 @@
 
     for s in asend:
         s.wait_recv()
-    tot = ploc[x] + ra[0] + ra[1] + ra[2]
+    for s in wsend[3:]:
+        s.start()
+    tot = pown[...] + ra[0].astype(F32) + ra[1].astype(F32) + ra[2].astype(F32)
     pa[0] = tot[:, :HALF]
     pa[1, :, pl.ds(0, XC - HALF)] = tot[:, HALF:]
     pa[1, :, pl.ds(XC - HALF, 2 * HALF - XC)] = jnp.zeros((R, 2 * HALF - XC), F32)
@@ -195,20 +208,25 @@
         b = remote(piece(pd, y), piece(pd, y), sd.at[k - 1], dd.at[k - 1], ydev(k))
         b.start()
         dsend.append(b)
+    for s in wsend[1:]:
+        s.wait_recv()
+    for s in wpass:
+        s.start()
     for s in dsend:
         s.wait_recv()
 
-    pe[x] = pd[...]
+    pb[...] = pd[...].astype(BF16)
+    pe[x] = pb[...]
     esend = []
     for k in (2, 1, 3):
-        b = remote(pd, pe.at[x], se.at[k - 1], de.at[k - 1], xdev(k))
+        b = remote(pb, pe.at[x], se.at[k - 1], de.at[k - 1], xdev(k))
         b.start()
         esend.append(b)
 
     for s in rsend:
         s.wait_recv()
     wown.wait()
-    for s in wsend:
+    for s in wsend[:1] + wpass:
         s.wait_recv()
 
     def grad(j, carry):
@@ -227,10 +245,9 @@
     def right(ch):
         tot = jnp.zeros((R, KD), F32)
         for h, n in ((0, HALF), (1, XC - HALF)):
-            ph, pl_ = split(pe[ch, h, :, :n])
+            ph = pe[ch, h, :, :n]
             rows = pl.ds(pl.multiple_of(ch * XC + h * HALF, 128), n)
-            r = mm(jnp.concatenate([ph, pl_], axis=0), mhi[rows], NN)
-            tot = tot + r[:R] + r[R:] + mm(ph, mlo[rows], NN)
+            tot = tot + mm(ph, mhi[rows], NN) + mm(ph, mlo[rows], NN)
         return tot
 
     qp = right(x)
@@ -249,9 +266,7 @@
     for ch in range(NX):
         for h, n in ((0, HALF), (1, XC - HALF)):
             b = pe[ch, h, :, :n]
-            gram = gram + mm(b, b, NT, HIGH)
-    row = lax.broadcasted_iota(jnp.int32, (R, KD), 0)
-    col = lax.broadcasted_iota(jnp.int32, (R, KD), 1)
+            gram = gram + mm(b, b, NT)
     aug[...] = jnp.where(col == row + R, 1.0, 0.0)
     aug[:, :R] = gram
 
@@ -289,13 +304,10 @@
     for ch in range(NX):
         for h, n in ((0, HALF), (1, XC - HALF)):
             cols = pl.ds(ch * XC + h * HALF, n)
-            p = mm(linv, pe[ch, h, :, :n], NN, HIGH)
+            p = mm(linv, pe[ch, h, :, :n].astype(F32), NN, HIGH)
             pf[:, cols] = p
             ph, pl_ = split(p)
-            at[pl.ds(0, R), cols] = ph
-            at[pl.ds(R, R), cols] = pl_
-            at[pl.ds(2 * R, R), cols] = ph
-    at[pl.ds(3 * R, R)] = jnp.zeros((R, D), BF16)
+            at[cols] = jnp.concatenate([ph, pl_, ph, jnp.zeros_like(ph)], axis=0).T
     put(at, at_out)
     put(pf, pf_out)
     for s in osend:
@@ -308,7 +320,7 @@
         q = q + ry[k]
     qf[...] = mm(linv, q, NN, HIGH) * (1.0 / (NX * NY * NZH))
     put(qf, qf_out)
-    for s in asend + bsend + csend + dsend + esend + fsend + hsend + ysend + wsend + gsend + rsend + osend:
+    for s in asend + bsend + csend + dsend + esend + fsend + hsend + ysend + wsend + wpass + gsend + rsend + osend:
         s.wait_send()
     for s in outs:
         s.wait()
@@ -323,7 +335,7 @@
     loads = []
     for h in range(3):
         part = pl.ds(h * 1536, 1536)
-        loads.append([load(at_in.at[:, part], at.at[:, part], 1 + 3 * h), load(mhi_in.at[part], mhi.at[part], 2 + 3 * h),
+        loads.append([load(at_in.at[part], at.at[part], 1 + 3 * h), load(mhi_in.at[part], mhi.at[part], 2 + 3 * h),
                       load(mlo_in.at[part], mlo.at[part], 3 + 3 * h)])
     through = [(qload, qf, qf_out), (load(ig_in, ig, 10), ig, ig_out), (load(pf_in, pf, 11), pf, pt_out)]
     copies = [pltpu.make_async_copy(b, o, sem.at[i]) for i, (l, b, o) in enumerate(through)]
@@ -337,7 +349,7 @@
 
         def finish(j, carry):
             rows = pl.ds(pl.multiple_of(h * 1536 + j * 256, 256), 256)
-            a = mm(at[:, rows], b4, TN)
+            a = mm(at[rows], b4, NN)
             err[rows] = ((mhi[rows].astype(F32) - a) + mlo[rows].astype(F32)).astype(BF16)
             return carry
         lax.fori_loop(0, 6, finish, 0)
@@ -358,18 +370,18 @@
     shape = jax.ShapeDtypeStruct
     parts = pl.pallas_call(
         kernel,
-        out_shape=(shape((KD, D), BF16), shape((D, KD), BF16), shape((D, KD), BF16),
+        out_shape=(shape((D, KD), BF16), shape((D, KD), BF16), shape((D, KD), BF16),
                    shape((TOK // 8, D), BF16), shape((R, D), F32), shape((R, KD), F32)),
         in_specs=[hbm] * 5,
         out_specs=[hbm] * 6,
         scratch_shapes=[
             pltpu.VMEM((TOK, D), BF16), pltpu.VMEM((TOK, KD), BF16), pltpu.VMEM((D, KD), BF16), pltpu.VMEM((R, KD), F32),
             pltpu.VMEM((SL, 1024), BF16), pltpu.VMEM((2, 128, 1024), BF16), pltpu.VMEM((256, SL), BF16), pltpu.VMEM((64, D), BF16),
-            pltpu.VMEM((NX, R, XC), F32), pltpu.VMEM((3, R, XC), F32), pltpu.VMEM((2, R, HALF), F32),
-            pltpu.VMEM((7, 8, HALF), F32), pltpu.VMEM((NZH, 8, HALF), F32), pltpu.VMEM((2, R, HALF), F32),
-            pltpu.VMEM((NX, 2, R, HALF), F32), pltpu.VMEM((D, KD), BF16), pltpu.VMEM((D, KD), BF16),
+            pltpu.VMEM((NX, R, XC), BF16), pltpu.VMEM((R, XC), F32), pltpu.VMEM((3, R, XC), BF16), pltpu.VMEM((2, R, HALF), F32),
+            pltpu.VMEM((7, 8, HALF), F32), pltpu.VMEM((NZH, 8, HALF), F32), pltpu.VMEM((2, R, HALF), F32), pltpu.VMEM((2, R, HALF), BF16),
+            pltpu.VMEM((NX, 2, R, HALF), BF16), pltpu.VMEM((D, KD), BF16), pltpu.VMEM((D, KD), BF16),
             pltpu.VMEM((NX, R, KD), F32), pltpu.VMEM((NZH, R, KD), F32), pltpu.VMEM((NY, R, KD), F32),
-            pltpu.VMEM((R, KD), F32), pltpu.VMEM((R, D), F32), pltpu.VMEM((KD, D), BF16), pltpu.VMEM((R, KD), F32),
+            pltpu.VMEM((R, KD), F32), pltpu.VMEM((R, D), F32), pltpu.VMEM((D, KD), BF16), pltpu.VMEM((R, KD), F32),
             dma(8), dma(3), dma(3), dma(7), dma(7), dma(2), dma(2), dma(7), dma(7), dma(3), dma(3),
             dma(3), dma(3), dma(2), dma(2), dma(7), dma(7), dma(9), dma(9), dma(3), dma(3), dma(3), dma(3), dma(3), dma(3), dma(6),
         ],
@@ -381,7 +393,7 @@
         out_shape=(shape((D, KD), BF16), shape((TOK // 8, D), BF16), shape((R, D), F32), shape((R, KD), F32)),
         in_specs=[hbm] * 6,
         out_specs=[hbm] * 4,
-        scratch_shapes=[pltpu.VMEM((KD, D), BF16), pltpu.VMEM((D, KD), BF16), pltpu.VMEM((D, KD), BF16), pltpu.VMEM((R, KD), F32),
+        scratch_shapes=[pltpu.VMEM((D, KD), BF16), pltpu.VMEM((D, KD), BF16), pltpu.VMEM((D, KD), BF16), pltpu.VMEM((R, KD), F32),
                         pltpu.VMEM((64, D), BF16), pltpu.VMEM((R, D), F32), pltpu.VMEM((D, KD), BF16), dma(6), dma(12)],
         compiler_params=pltpu.CompilerParams(vmem_limit_bytes=60 << 20),
         name="finish",

time: 86.6 us -> 70.5 us (0.81)
  the two profiles are of different devices: /device:TPU:64 before, /device:TPU:2 now
where the time goes in v3:
time: 70.5 us; the launch traced here: 70.3 us
  Pallas kernels  69.7 us (99%)
    pallas_call x1, Pallas kernels, shards(): pl.pallas_call(kernel, out_shape=(shape((D, KD), BF16), shape((D, KD), BF...  64.8 us
    pallas_call x1, Pallas kernels, shards(): pl.pallas_call(last, out_shape=(shape((D, KD), BF16), shape((TOK // 8, D)...  4.88 us

profile of v3, /device:TPU:2, one launch (start us, length us, event | category | flops | bytes accessed | tf_op | source)
XLA Modules:
  0.0 70.3 jit_solution(9329543015317075970)
XLA Ops:
  0.6 64.8 %powersgd.1 = (bf16[4608,128]{1,0:T(8,128)(2,1)}, bf16[4608,128]{1,0:T(8,128)(2,1)}, bf16[4608,128]{1,0:T(8,128)(2,1)}, bf16[64,4608]{1,0:T(8,128)(2,1)}, f32[32,4608]{1,0:T(8,128)}, /*index=5*/f32[32,128]{1,0:T(8,128)}) custom-call(bf16[512,4608]{1,0:T(8,128)(2,1)} %x_hbm.1, bf16[512,128]{1,0:T(8,128)(2,1)} %g_hbm.1, bf16[4608,128]{1,0:T(8,128)(2,1)} %w_hbm.1, ...), custom_call_target="tpu_custom_call" | custom-call | tf_op jit(solution)/shard_map/powersgd/pallas_call | solution.py:371
  65.4 4.9 %finish.1 = (bf16[4608,128]{1,0:T(8,128)(2,1)}, bf16[64,4608]{1,0:T(8,128)(2,1)}, f32[32,4608]{1,0:T(8,128)}, f32[32,128]{1,0:T(8,128)}) custom-call(bf16[4608,128]{1,0:T(8,128)(2,1)} %get-tuple-element.14.at_in, bf16[4608,128]{1,0:T(8,128)(2,1)} %get-tuple-element.15.mhi_in, bf16[4608,128]{1,0:T(8,128)(2,1)} %get-tuple-element.16.mlo_in, ...), custom_call_target="tpu_custom_call" | custom-call | tf_op jit(solution)/shard_map/finish/pallas_call | solution.py:391

commit v4 on v3

--- a/solution.py
+++ b/solution.py
@@ -347,13 +347,9 @@
         for l in loads[h]:
             l.wait()
 
-        def finish(j, carry):
-            rows = pl.ds(pl.multiple_of(h * 1536 + j * 256, 256), 256)
-            a = mm(at[rows], b4, NN)
-            err[rows] = ((mhi[rows].astype(F32) - a) + mlo[rows].astype(F32)).astype(BF16)
-            return carry
-        lax.fori_loop(0, 6, finish, 0)
         part = pl.ds(h * 1536, 1536)
+        a = mm(at[part], b4, NN)
+        err[part] = ((mhi[part].astype(F32) - a) + mlo[part].astype(F32)).astype(BF16)
         c = pltpu.make_async_copy(err.at[part], err_out.at[part], sem.at[3 + h])
         c.start()
         copies.append(c)

time: 70.5 us -> 69.4 us (0.984)
  Pallas kernels: 69.7 us -> 68.5 us
    pallas_call x1, Pallas kernels: 4.88 us -> 3.73 us  [shards(): pl.pallas_call(last, out_shape=(shape((D, KD), BF16), shape((TOK // 8, D)...]
where the time goes in v4:
time: 69.4 us; the launch traced here: 69.1 us
  Pallas kernels  68.5 us (99%)
    pallas_call x1, Pallas kernels, shards(): pl.pallas_call(kernel, out_shape=(shape((D, KD), BF16), shape((D, KD), BF...  64.8 us
    pallas_call x1, Pallas kernels, shards(): pl.pallas_call(last, out_shape=(shape((D, KD), BF16), shape((TOK // 8, D)...  3.73 us

profile of v4, /device:TPU:2, one launch (start us, length us, event | category | flops | bytes accessed | tf_op | source)
XLA Modules:
  0.0 69.1 jit_solution(9146903344062431136)
XLA Ops:
  0.6 64.8 %powersgd.1 = (bf16[4608,128]{1,0:T(8,128)(2,1)}, bf16[4608,128]{1,0:T(8,128)(2,1)}, bf16[4608,128]{1,0:T(8,128)(2,1)}, bf16[64,4608]{1,0:T(8,128)(2,1)}, f32[32,4608]{1,0:T(8,128)}, /*index=5*/f32[32,128]{1,0:T(8,128)}) custom-call(bf16[512,4608]{1,0:T(8,128)(2,1)} %x_hbm.1, bf16[512,128]{1,0:T(8,128)(2,1)} %g_hbm.1, bf16[4608,128]{1,0:T(8,128)(2,1)} %w_hbm.1, ...), custom_call_target="tpu_custom_call" | custom-call | tf_op jit(solution)/shard_map/powersgd/pallas_call | solution.py:367
  65.4 3.7 %finish.1 = (bf16[4608,128]{1,0:T(8,128)(2,1)}, bf16[64,4608]{1,0:T(8,128)(2,1)}, f32[32,4608]{1,0:T(8,128)}, f32[32,128]{1,0:T(8,128)}) custom-call(bf16[4608,128]{1,0:T(8,128)(2,1)} %get-tuple-element.14.at_in, bf16[4608,128]{1,0:T(8,128)(2,1)} %get-tuple-element.15.mhi_in, bf16[4608,128]{1,0:T(8,128)(2,1)} %get-tuple-element.16.mlo_in, ...), custom_call_target="tpu_custom_call" | custom-call | tf_op jit(solution)/shard_map/finish/pallas_call | solution.py:387

commit v5 on v4

--- a/solution.py
+++ b/solution.py
@@ -27,6 +27,15 @@
 def split(a):
     hi = a.astype(BF16)
     return hi, (a - hi.astype(F32)).astype(BF16)
+
+
+def factor(a):
+    row = lax.broadcasted_iota(jnp.int32, (R, KD), 0)
+    for k in range(R):
+        s = 1.0 / jnp.sqrt(a[k:k + 1, k:k + 1])
+        rn = a[k:k + 1] * s
+        a = jnp.where(row == k, rn, a - jnp.where(row > k, a[:, k:k + 1] * s, 0.0) * rn)
+    return a
 
 
 def device(x, y, z, c):
@@ -92,12 +101,7 @@
     q0 = qv[...]
     aug[...] = jnp.where(col == row + R, 1.0, 0.0)
     aug[:, :R] = mm(q0, q0, NT, HIGH)
-    a = aug[...]
-    for k in range(R):
-        s = lax.rsqrt(a[k:k + 1, k:k + 1])
-        rn = a[k:k + 1] * s
-        a = jnp.where(row == k, rn, a - jnp.where(row > k, a[:, k:k + 1] * s, 0.0) * rn)
-    aug[...] = a
+    aug[...] = factor(aug[...])
     qh, ql = split(mm(aug[:, R:2 * R], q0, NN, HIGH))
     q2 = jnp.concatenate([qh, ql], axis=0)
     gq = mm(q2, gv[...], NT)
@@ -151,15 +155,12 @@
         mhi[rows] = h
         mlo[rows] = l
         return carry
-    lax.fori_loop(0, 18, merge, 0)
     outs = []
 
     def put(src, dst):
         cp = pltpu.make_async_copy(src, dst, osem.at[len(outs)])
         cp.start()
         outs.append(cp)
-    put(mhi, mhi_out)
-    put(mlo, mlo_out)
 
     for s in asend:
         s.wait_recv()
@@ -174,7 +175,7 @@
         return ref.at[j // 4, pl.ds(pl.multiple_of(lax.rem(j, 4) * 8, 8), 8)]
 
     bsend = []
-    for k in range(1, 8):
+    for k in (4, 3, 5, 2, 6, 1, 7):
         b = remote(piece(pa, lax.rem(y + k, NY)), rb.at[k - 1], sb.at[k - 1], db.at[k - 1], ydev(k))
         b.start()
         bsend.append(b)
@@ -187,6 +188,7 @@
     for s in rsend:
         s.start()
 
+    lax.fori_loop(0, 9, merge, 0)
     for s in bsend:
         s.wait_recv()
     own = piece(pa, y)[...]
@@ -199,12 +201,15 @@
         b = remote(rc.at[zh], rc.at[zh], sc.at[k], dc.at[k], zdev(dz_, c))
         b.start()
         csend.append(b)
+    lax.fori_loop(9, 18, merge, 0)
+    put(mhi, mhi_out)
+    put(mlo, mlo_out)
     for s in csend:
         s.wait_recv()
     piece(pd, y)[...] = rc[0] + rc[1] + rc[2]
 
     dsend = []
-    for k in range(1, 8):
+    for k in (4, 3, 5, 2, 6, 1, 7):
         b = remote(piece(pd, y), piece(pd, y), sd.at[k - 1], dd.at[k - 1], ydev(k))
         b.start()
         dsend.append(b)
@@ -270,16 +275,8 @@
     aug[...] = jnp.where(col == row + R, 1.0, 0.0)
     aug[:, :R] = gram
 
-    def factor(k, carry):
-        a = aug[...]
-        r = jnp.sum(jnp.where(row == k, a, 0.0), axis=0, keepdims=True)
-        cl = jnp.sum(jnp.where(col == k, a, 0.0), axis=1, keepdims=True)
-        pivot = jnp.sum(jnp.where(col[:1] == k, r, 0.0), axis=1, keepdims=True)
-        s = 1.0 / jnp.sqrt(pivot)
-        rn = r * s
-        aug[...] = jnp.where(row == k, rn, jnp.where(row > k, a - (cl * s) * rn, a))
-        return carry
-
+    aug[...] = factor(aug[...])
+    linv = aug[:, R:2 * R]
     for s in fsend:
         s.wait_recv()
     rz[zh] = rx[0] + rx[1] + rx[2] + rx[3]
@@ -289,18 +286,6 @@
         b = remote(rz.at[zh], rz.at[zh], sz.at[k], dz.at[k], zdev(dz_, c))
         b.start()
         hsend.append(b)
-    lax.fori_loop(0, 16, factor, 0)
-    for s in hsend:
-        s.wait_recv()
-    ry[y] = rz[0] + rz[1] + rz[2]
-
-    ysend = []
-    for k in range(1, 8):
-        b = remote(ry.at[y], ry.at[y], sy.at[k - 1], dy.at[k - 1], ydev(k))
-        b.start()
-        ysend.append(b)
-    lax.fori_loop(16, R, factor, 0)
-    linv = aug[:, R:2 * R]
     for ch in range(NX):
         for h, n in ((0, HALF), (1, XC - HALF)):
             cols = pl.ds(ch * XC + h * HALF, n)
@@ -310,6 +295,15 @@
             at[cols] = jnp.concatenate([ph, pl_, ph, jnp.zeros_like(ph)], axis=0).T
     put(at, at_out)
     put(pf, pf_out)
+    for s in hsend:
+        s.wait_recv()
+    ry[y] = rz[0] + rz[1] + rz[2]
+
+    ysend = []
+    for k in (4, 3, 5, 2, 6, 1, 7):
+        b = remote(ry.at[y], ry.at[y], sy.at[k - 1], dy.at[k - 1], ydev(k))
+        b.start()
+        ysend.append(b)
     for s in osend:
         s.wait_recv()
     put(igbuf, ig_out)

time: 69.4 us -> 68.9 us (level)
  the two profiles are of different devices: /device:TPU:2 before, /device:TPU:8 now
where the time goes in v5:
time: 68.9 us; the launch traced here: 68.7 us
  Pallas kernels  68 us (99%)
    pallas_call x1, Pallas kernels, shards(): pl.pallas_call(kernel, out_shape=(shape((D, KD), BF16), shape((D, KD), BF...  64.3 us
    pallas_call x1, Pallas kernels, shards(): pl.pallas_call(last, out_shape=(shape((D, KD), BF16), shape((TOK // 8, D)...  3.73 us

profile of v5, /device:TPU:8, one launch (start us, length us, event | category | flops | bytes accessed | tf_op | source)
XLA Modules:
  0.0 68.7 jit_solution(17071256663446982676)
XLA Ops:
  0.6 64.3 %powersgd.1 = (bf16[4608,128]{1,0:T(8,128)(2,1)}, bf16[4608,128]{1,0:T(8,128)(2,1)}, bf16[4608,128]{1,0:T(8,128)(2,1)}, bf16[64,4608]{1,0:T(8,128)(2,1)}, f32[32,4608]{1,0:T(8,128)}, /*index=5*/f32[32,128]{1,0:T(8,128)}) custom-call(bf16[512,4608]{1,0:T(8,128)(2,1)} %x_hbm.1, bf16[512,128]{1,0:T(8,128)(2,1)} %g_hbm.1, bf16[4608,128]{1,0:T(8,128)(2,1)} %w_hbm.1, ...), custom_call_target="tpu_custom_call" | custom-call | tf_op jit(solution)/shard_map/powersgd/pallas_call | solution.py:361
  64.9 3.7 %finish.1 = (bf16[4608,128]{1,0:T(8,128)(2,1)}, bf16[64,4608]{1,0:T(8,128)(2,1)}, f32[32,4608]{1,0:T(8,128)}, f32[32,128]{1,0:T(8,128)}) custom-call(bf16[4608,128]{1,0:T(8,128)(2,1)} %get-tuple-element.14.at_in, bf16[4608,128]{1,0:T(8,128)(2,1)} %get-tuple-element.15.mhi_in, bf16[4608,128]{1,0:T(8,128)(2,1)} %get-tuple-element.16.mlo_in, ...), custom_call_target="tpu_custom_call" | custom-call | tf_op jit(solution)/shard_map/finish/pallas_call | solution.py:381
